TPU v7x, 32 devices: a whole 2x2x4 slice. The times are simulated.
32 devices in a mesh: lat: 4 (over z), lon: 4 (over y, core), buf: 2 (over x).
Axes of the slice: x: 2, y: 2, z: 4, core: 2. Of those that a mesh axis runs over, the one named last changes fastest.
Arguments:
- store: bfloat16 [8, 64, 64, 1725], P('buf', ('lat', 'lon')), may hold values from -6 to 6
- sample_index: int32 [6], replicated, may hold values from 0 to 7, as said below
- region_ids: int32 [64, 64], replicated, may hold values from 0 to 2
- w_embed: bfloat16 [1725, 512], replicated, may hold values from -0.15625 to 0.15625
- attn_gain: float32 [512], replicated, may hold values from 0.1 to 1.9
- w_qkv: bfloat16 [512, 1536], replicated, may hold values from -8 to 8
- w_out: bfloat16 [512, 512], replicated, may hold values from -0.25 to 0.25
- out_gain: float32 [512], replicated, may hold values from 0.1 to 1.9
- w_dec: bfloat16 [512, 1725], replicated, may hold values from -0.25 to 0.25
Outputs:
- new_store: bfloat16 [8, 64, 64, 1725], P('buf', ('lat', 'lon'))
Inputs may be any that keep to these rules, and one draw needn't show every extreme that they name: `sample_index`: distinct slot numbers.
All inputs are finite; a program needn't handle non-finite values.
Results may differ from a plain program's by a relative error of at most 0.007.
Values may be sent and summed in bfloat16 or wider, within the bound.
A program may use at most 128 MiB of HBM per device.

v0:
```python
import math

import jax
import jax.numpy as jnp
from jax import lax
from jax.experimental import pallas as pl
from jax.experimental.pallas import tpu as pltpu
from jax.sharding import PartitionSpec as P

D = 512
HEADS = 8
HDIM = 64
WIN = 8
HALF = WIN // 2
VMEM_LIMIT = 56 * 1024 * 1024
PICK_LIMIT = 4 * 1024 * 1024


def with_halo(array, sides, width):
    for axis, dim in sides:
        devices, length = (lax.axis_size(axis), array.shape[dim])
        up = [(i, (i + 1) % devices) for i in range(devices)]
        down = [(j, i) for i, j in up]
        last = lax.slice_in_dim(array, length - width, length, axis=dim)
        leading = lax.slice_in_dim(array, 0, width, axis=dim)
        before = lax.ppermute(last, axis, up)
        after = lax.ppermute(leading, axis, down)
        array = jnp.concatenate([before, array, after], axis=dim)
    return array


def layer_norm(values, gain_row):
    center = jnp.mean(values, axis=-1, keepdims=True)
    spread = jnp.mean(jnp.square(values - center), axis=-1, keepdims=True)
    return (values - center) * lax.rsqrt(spread + 1e-05) * gain_row


def window_mix(windows, regions):
    scores = jnp.einsum(
        "bwqhd,bwkhd->bwhqk",
        windows[:, :, :, 0],
        windows[:, :, :, 1],
        preferred_element_type=jnp.float32,
    ) / math.sqrt(HDIM)
    visible = (regions[:, :, None] == regions[:, None, :])[None, :, None]
    scores = jnp.where(visible, scores, -1e30)
    highest = jnp.max(scores, axis=-1, keepdims=True)
    expo_terms = jnp.where(visible, jnp.exp(scores - highest), 0.0)
    weights = (expo_terms / jnp.sum(expo_terms, axis=-1, keepdims=True)).astype(jnp.bfloat16)
    return jnp.einsum(
        "bwhqk,bwkhd->bwqhd", weights, windows[:, :, :, 2], preferred_element_type=jnp.float32
    ).astype(jnp.bfloat16)


def local_tiles(store, sample_index, region_ids, w_embed, attn_gain, w_qkv, w_out, out_gain, w_dec):
    lon_count = lax.axis_size("lon")
    slots_here, rows_here, width_all, patch_len = store.shape
    patch_cols = width_all // lon_count
    patch_rows = rows_here * lon_count
    half_win = WIN // 2
    ext_rows = patch_rows + WIN
    ext_cols = patch_cols + WIN
    own_slots = lax.axis_index("buf") * slots_here + jnp.arange(slots_here, dtype=jnp.int32)
    matches = own_slots[:, None] == sample_index[None, :]
    occupied = jnp.any(matches, axis=1)
    local_rows = store.reshape(slots_here, 1, rows_here, lon_count, patch_cols, patch_len)
    tile_data = lax.all_to_all(local_rows, "lon", split_axis=3, concat_axis=1, tiled=True)
    patches = tile_data.reshape(-1, patch_len)
    embedded = jnp.dot(patches, w_embed, preferred_element_type=jnp.float32).astype(jnp.bfloat16)
    normed = layer_norm(embedded.astype(jnp.float32), attn_gain).astype(jnp.bfloat16)
    normed = normed.reshape(slots_here, patch_rows, patch_cols, D)
    widened = with_halo(normed, (("lat", 1), ("lon", 2)), half_win)
    projected = jnp.dot(widened.reshape(-1, D), w_qkv, preferred_element_type=jnp.float32).astype(
        jnp.bfloat16
    )
    windows = projected.reshape(
        slots_here, ext_rows // WIN, WIN, ext_cols // WIN, WIN, 3, HEADS, HDIM
    )
    windows = windows.transpose(0, 1, 3, 2, 4, 5, 6, 7).reshape(
        slots_here, -1, WIN * WIN, 3, HEADS, HDIM
    )
    total_rows, total_cols = region_ids.shape
    row_pick = (
        lax.axis_index("lat") * patch_rows - half_win + jnp.arange(ext_rows, dtype=jnp.int32)
    ) % total_rows
    col_pick = (
        lax.axis_index("lon") * patch_cols - half_win + jnp.arange(ext_cols, dtype=jnp.int32)
    ) % total_cols
    local_regions = jnp.take(jnp.take(region_ids, row_pick, axis=0), col_pick, axis=1)
    region_windows = (
        local_regions.reshape(ext_rows // WIN, WIN, ext_cols // WIN, WIN)
        .transpose(0, 2, 1, 3)
        .reshape(-1, WIN * WIN)
    )
    mixed_heads = window_mix(windows, region_windows)
    placed = mixed_heads.reshape(slots_here, ext_rows // WIN, ext_cols // WIN, WIN, WIN, D)
    placed = placed.transpose(0, 1, 3, 2, 4, 5).reshape(slots_here, ext_rows, ext_cols, D)
    placed = placed[:, half_win : half_win + patch_rows, half_win : half_win + patch_cols].reshape(
        -1, D
    )
    updated = embedded.astype(jnp.float32) + jnp.dot(
        placed, w_out, preferred_element_type=jnp.float32
    )
    final_norm = layer_norm(updated, out_gain).astype(jnp.bfloat16)
    predicted = (
        patches.astype(jnp.float32) + jnp.dot(final_norm, w_dec, preferred_element_type=jnp.float32)
    ).astype(jnp.bfloat16)
    outgoing = predicted.reshape(slots_here, lon_count, rows_here, 1, patch_cols, patch_len)
    returned = lax.all_to_all(outgoing, "lon", split_axis=1, concat_axis=3, tiled=True)
    strip_data = returned.reshape(slots_here, rows_here, width_all, patch_len)
    return jnp.where(occupied[:, None, None, None], strip_data, store)


def to_windows(values):
    rows, cols = HALF, values.shape[0] // HALF
    parts = [pltpu.roll(values[cols * i : cols * (i + 1)], cols - HALF, 0) for i in range(rows)]
    return jnp.concatenate(
        [parts[i][WIN * c : WIN * (c + 1)] for c in range(cols // WIN) for i in range(rows)], axis=0
    )


def from_windows(values):
    rows, cols = HALF, values.shape[0] // HALF
    parts = []
    for i in range(rows):
        line = jnp.concatenate(
            [
                values[WIN * (rows * c + i) : WIN * (rows * c + i + 1)]
                for c in range(cols // WIN)
            ],
            axis=0,
        )
        parts.append(pltpu.roll(line, HALF, 0))
    return jnp.concatenate(parts, axis=0)


def embed_slot(patches, w_embed, gain):
    embedded = jnp.dot(patches, w_embed, preferred_element_type=jnp.float32).astype(jnp.bfloat16)
    embedded = to_windows(embedded.astype(jnp.float32))
    normed = layer_norm(embedded, gain).astype(jnp.bfloat16)
    return embedded.astype(jnp.bfloat16), normed


NT = (((1,), (1,)), ((), ()))
TN = (((0,), (0,)), ((), ()))
GROUP = 4
WIDE = GROUP * HDIM
PER = WIN * HALF


def attend_slot(query, kv_own, kv_other, q_regions, k_regions):
    shape = (GROUP * PER, WIDE)
    pick = (
        lax.broadcasted_iota(jnp.int32, shape, 0) // PER
        == lax.broadcasted_iota(jnp.int32, shape, 1) // HDIM
    )
    head_mask = jnp.where(pick, 1.0, 0.0).astype(jnp.bfloat16)
    windows = query.shape[0] // PER
    kvs, scores, weights, mixed = [], [], [], []
    for c in range(windows):
        at = slice(PER * c, PER * (c + 1))
        kvs.append(jnp.concatenate([kv_own[at], kv_other[at]], axis=0))
        for g in range(HEADS // GROUP):
            cols = slice(WIDE * g, WIDE * (g + 1))
            queries = jnp.concatenate([query[at, cols]] * GROUP, axis=0) * head_mask
            scores.append(
                lax.dot_general(kvs[c][:, cols], queries, NT, preferred_element_type=jnp.float32)
            )
    for c in range(windows):
        seen = k_regions[:, c : c + 1] == q_regions[c : c + 1, :]
        for g in range(HEADS // GROUP):
            part = jnp.where(seen, scores[2 * c + g], -1e30)
            expo = jnp.exp(part - jnp.max(part, axis=0, keepdims=True))
            total = jnp.sum(expo, axis=0, keepdims=True)
            weights.append((expo * (1.0 / total)).astype(jnp.bfloat16))
    for c in range(windows):
        groups = []
        for g in range(HEADS // GROUP):
            heads = lax.dot_general(
                weights[2 * c + g],
                kvs[c][:, D + WIDE * g : D + WIDE * (g + 1)],
                TN,
                preferred_element_type=jnp.float32,
            )
            heads = jnp.where(pick, heads, 0.0)
            total = heads[:PER]
            for h in range(1, GROUP):
                total = total + heads[PER * h : PER * (h + 1)]
            groups.append(total)
        mixed.append(jnp.concatenate(groups, axis=1).astype(jnp.bfloat16))
    return jnp.concatenate(mixed, axis=0)


def region_tables(own, far):
    rows, cols = own.shape
    windows = cols // WIN
    lines = [own[i : i + 1] for i in range(rows)] + [far[i : i + 1] for i in range(rows)]
    wide = jnp.concatenate([jnp.broadcast_to(line, (WIN, cols)) for line in lines], axis=0)
    row = lax.broadcasted_iota(jnp.int32, wide.shape, 0)
    col = lax.broadcasted_iota(jnp.int32, wide.shape, 1)
    kept = jnp.where((col + WIN - HALF) % WIN == row % WIN, wide, 0.0).astype(jnp.bfloat16)
    place = (lax.broadcasted_iota(jnp.int32, (windows, cols), 1) + cols - HALF) % cols // WIN
    here = place == lax.broadcasted_iota(jnp.int32, (windows, cols), 0)
    here = jnp.where(here, 1.0, 0.0).astype(jnp.bfloat16)
    k_regions = lax.dot_general(kept, here, NT, preferred_element_type=jnp.float32)
    q_rows = jnp.concatenate([kept[:PER]] * GROUP, axis=0)
    q_regions = lax.dot_general(here, q_rows, NT, preferred_element_type=jnp.float32)
    return q_regions, k_regions


def finish_part(embedded, mixed, w_out, gain):
    updated = embedded.astype(jnp.float32) + jnp.dot(
        mixed, w_out, preferred_element_type=jnp.float32
    )
    return layer_norm(updated, gain)


def decode_slot(patches, final, w_dec_t):
    return (
        patches.astype(jnp.float32)
        + lax.dot_general(
            final, w_dec_t, (((1,), (1,)), ((), ())), preferred_element_type=jnp.float32
        )
    ).astype(jnp.bfloat16)


def fused_kernel(
    sample_ref,
    region_ref,
    a_gain_ref,
    o_gain_ref,
    store_ref,
    w_embed_ref,
    w_qkv_ref,
    w_out_ref,
    w_dec_ref,
    new_ref,
    patches,
    w_embed,
    w_qkv,
    w_out,
    w_dec,
    embedded,
    own,
    far,
    own_qkv,
    finals,
    slot_sems,
    weight_sems,
    send_sems,
    recv_sems,
):
    slots, rows_here, cols, patch_len = store_ref.shape
    lon_count = lax.axis_size("lon")
    strips = lax.axis_size("lat") * lon_count
    mine = lax.axis_index("lat") * lon_count + lax.axis_index("lon")
    other = lax.rem(mine + 2 * lax.rem(mine, 2) - 1 + strips, strips)
    partner = {"lat": lax.div(other, lon_count), "lon": lax.rem(other, lon_count)}

    def slot_in(s):
        return pltpu.make_async_copy(store_ref.at[s], patches.at[s], slot_sems.at[s])

    tokens = rows_here * cols
    half = tokens // 2
    halves = [pl.ds(half * h, half) for h in range(2)]

    def send(k, h):
        return pltpu.make_async_remote_copy(
            src_ref=own.at[k, halves[h]],
            dst_ref=far.at[k, halves[h]],
            send_sem=send_sems.at[k, h],
            recv_sem=recv_sems.at[k, h],
            device_id=partner,
            device_id_type=pl.DeviceIdType.MESH,
        )

    weights = [
        pltpu.make_async_copy(src, dst, weight_sems.at[i])
        for i, (src, dst) in enumerate(
            ((w_embed_ref, w_embed), (w_qkv_ref, w_qkv), (w_out_ref, w_out), (w_dec_ref, w_dec))
        )
    ]
    weights[0].start()
    slot_in(0).start()

    barrier = pltpu.get_barrier_semaphore()
    pl.semaphore_signal(
        barrier, inc=1, device_id=partner, device_id_type=pl.DeviceIdType.MESH
    )
    q_regions, k_regions = region_tables(
        region_ref[pl.ds(mine * HALF, HALF), :].astype(jnp.float32),
        region_ref[pl.ds(other * HALF, HALF), :].astype(jnp.float32),
    )
    pl.semaphore_wait(barrier, 1)
    weights[0].wait()
    slot_in(0).wait()
    for s in range(1, slots):
        slot_in(s).start()
    for copy in weights[1:]:
        copy.start()

    @pl.loop(0, slots)
    def _(k):
        @pl.when(k > 0)
        def _():
            slot_in(k).wait()

        flat = patches[k].reshape(tokens, patch_len)
        embedded[k], own[k] = embed_slot(flat, w_embed[...], a_gain_ref[...])
        for h in range(2):
            send(k, h).start()

    weights[1].wait()

    @pl.loop(0, slots)
    def _(k):
        query = jnp.dot(own[k], w_qkv[:, :D], preferred_element_type=jnp.float32)
        own_qkv[k, :, :D] = (query * (1.0 / math.sqrt(HDIM))).astype(jnp.bfloat16)
        own_qkv[k, :, D:] = jnp.dot(
            own[k], w_qkv[:, D:], preferred_element_type=jnp.float32
        ).astype(jnp.bfloat16)

    weights[2].wait()
    weights[3].wait()
    windows = tokens // PER

    @pl.loop(0, slots)
    def _(k):
        for h in range(2):
            send(k, h).wait()
            at = slice(half * h, half * (h + 1))
            here = slice(windows // 2 * h, windows // 2 * (h + 1))
            kv_other = jnp.dot(far[k, at], w_qkv[:, D:], preferred_element_type=jnp.float32)
            mixed = attend_slot(
                own_qkv[k, at, :D],
                own_qkv[k, at, D:],
                kv_other.astype(jnp.bfloat16),
                q_regions[here],
                k_regions[:, here],
            )
            finals[at] = finish_part(embedded[k, at], mixed, w_out[...], o_gain_ref[...])
        final = from_windows(finals[...]).astype(jnp.bfloat16)
        slot = lax.axis_index("buf") * slots + k
        taken = sample_ref[0] == slot
        for b in range(1, sample_ref.shape[0]):
            taken = jnp.logical_or(taken, sample_ref[b] == slot)
        final = jnp.where(taken, final, jnp.zeros_like(final))
        flat = patches[k].reshape(tokens, patch_len)
        new_ref[k] = decode_slot(flat, final, w_dec[...]).reshape(rows_here, cols, patch_len)


def place_kernel(result_ref, new_ref, sems):
    slots, rows = new_ref.shape[:2]
    copies = [
        pltpu.make_async_copy(result_ref.at[s, i], new_ref.at[s, i], sems.at[s, i])
        for s in range(slots)
        for i in range(rows)
    ]
    for copy in copies:
        copy.start()
    for copy in copies:
        copy.wait()


def local_strips(
    store, sample_index, region_ids, w_embed, attn_gain, w_qkv, w_out, out_gain, w_dec
):
    slots, rows_here, cols, patch_len = store.shape
    tokens = rows_here * cols
    held = lambda *shape: pltpu.VMEM(shape, jnp.bfloat16)
    vmem = pl.BlockSpec(memory_space=pltpu.VMEM)
    hbm = pl.BlockSpec(memory_space=pl.ANY)
    result = pl.pallas_call(
        fused_kernel,
        in_specs=[pl.BlockSpec(memory_space=pltpu.SMEM), vmem, vmem, vmem] + [hbm] * 5,
        out_specs=vmem,
        out_shape=pltpu.VMEM(store.shape, store.dtype),
        scratch_shapes=[
            held(*store.shape),
            held(*w_embed.shape),
            held(*w_qkv.shape),
            held(*w_out.shape),
            held(*w_dec.shape[::-1]),
            held(slots, tokens, D),
            held(slots, tokens, D),
            held(slots, tokens, D),
            held(slots, tokens, 3 * D),
            pltpu.VMEM((tokens, D), jnp.float32),
            pltpu.SemaphoreType.DMA((slots,)),
            pltpu.SemaphoreType.DMA((4,)),
            pltpu.SemaphoreType.DMA((slots, 2)),
            pltpu.SemaphoreType.DMA((slots, 2)),
        ],
        compiler_params=pltpu.CompilerParams(
            vmem_limit_bytes=VMEM_LIMIT, collective_id=0, has_side_effects=True
        ),
    )(
        sample_index,
        region_ids,
        attn_gain[None],
        out_gain[None],
        store,
        w_embed,
        w_qkv,
        w_out,
        w_dec.T,
    )
    return pl.pallas_call(
        place_kernel,
        in_specs=[hbm],
        out_specs=hbm,
        out_shape=jax.ShapeDtypeStruct(store.shape, store.dtype),
        scratch_shapes=[pltpu.SemaphoreType.DMA((slots, rows_here))],
        compiler_params=pltpu.CompilerParams(vmem_limit_bytes=PICK_LIMIT),
    )(result)


def local(store, *rest):
    return (local_strips if store.shape[1] == HALF else local_tiles)(store, *rest)


def solution(mesh):
    return jax.shard_map(
        local,
        mesh=mesh,
        in_specs=(P("buf", ("lat", "lon"), None, None), P(), P(), P(), P(), P(), P(), P(), P()),
        out_specs=P("buf", ("lat", "lon"), None, None),
        check_vma=False,
    )
```

profile of v0, /device:TPU:1, one launch (start us, length us, event | category | flops | bytes accessed | tf_op | source)
XLA Modules:
  0.0 33.8 jit_solution(819630507097990058)
XLA Ops:
  0.0 31.8 %shard_map.91.result_ref = bf16[4,4,64,1725]{3,2,1,0:T(8,128)(2,1)S(1)} custom-call(s32[6]{0:T(128)} %sample_ref.1, s32[64,64]{1,0:T(8,128)} %region_ref.1, f32[1,512]{1,0:T(1,128)} %bitcast.4, f32[1,512]{1,0:T(1,128)} %bitcast.5, bf16[4,4,64,1725]{3,2,1,0:T(8,128)(2,1)} %store_ref.1, bf16[1725,512]{1,0:T(8,128)(2,1)} %w_embed_ref.1, ...), custom_call_target="tpu_custom_call" | custom-call | tf_op jit(solution)/shard_map/pallas_call | solution.py:373
  31.8 2.0 %shard_map.92 = bf16[4,4,64,1725]{3,2,1,0:T(8,128)(2,1)} custom-call(bf16[4,4,64,1725]{3,2,1,0:T(8,128)(2,1)S(1)} %shard_map.91.result_ref), custom_call_target="tpu_custom_call" | custom-call | tf_op jit(solution)/shard_map/pallas_call | solution.py:408
where the time goes:
time: 34 us; the launch traced here: 33.8 us
  Pallas kernels  33.8 us (99%)
    pallas_call x1, Pallas kernels, local_strips(): pl.pallas_call(fused_kernel, in_specs=[pl.BlockSpec(memory_space=pltpu.SM...  31.8 us
    pallas_call x1, Pallas kernels, local_strips(): pl.pallas_call(place_kernel, in_specs=[hbm], out_specs=hbm, out_shape=jax...  1.96 us

commit v1 on v0

--- a/solution.py
+++ b/solution.py
@@ -12,8 +12,9 @@
 HDIM = 64
 WIN = 8
 HALF = WIN // 2
-VMEM_LIMIT = 56 * 1024 * 1024
-PICK_LIMIT = 4 * 1024 * 1024
+VMEM_LIMIT = 40 * 1024 * 1024
+LAST_LIMIT = 40 * 1024 * 1024
+FIRST_LIMIT = 56 * 1024 * 1024
 
 
 def with_halo(array, sides, width):
@@ -224,29 +225,82 @@
     ).astype(jnp.bfloat16)
 
 
-def fused_kernel(
+MESH = pl.DeviceIdType.MESH
+UNIT_A, UNIT_C, UNIT_D, UNIT_B = range(4)
+
+
+def slot_order(sample_ref, slots):
+    first = lax.axis_index("buf") * slots
+    taken = []
+    for s in range(slots):
+        hit = sample_ref[0] == first + s
+        for b in range(1, sample_ref.shape[0]):
+            hit = jnp.logical_or(hit, sample_ref[b] == first + s)
+        taken.append(hit.astype(jnp.int32))
+    count = sum(taken)
+    places, before = [], jnp.int32(0)
+    for s in range(slots):
+        places.append(jnp.where(taken[s] == 1, before, count + s - before))
+        before = before + taken[s]
+    order = [
+        sum(jnp.where(places[s] == j, jnp.int32(s), 0) for s in range(slots)) for j in range(slots)
+    ]
+    return [order[j] for j in (0, 2, 3, 1)], count
+
+
+def first_kernel(
+    sample_ref, gain_ref, store_ref, w_embed_ref, w_embed, grabbed, embedded, own, sems
+):
+    slots, rows_here, cols, patch_len = store_ref.shape
+    order, _ = slot_order(sample_ref, slots)
+    weight = pltpu.make_async_copy(w_embed_ref, w_embed, sems.at[0])
+    fetch_a = pltpu.make_async_copy(store_ref.at[order[UNIT_A]], grabbed.at[0], sems.at[1])
+    fetch_d = pltpu.make_async_copy(store_ref.at[order[UNIT_D]], grabbed.at[1], sems.at[2])
+    weight.start()
+    fetch_a.start()
+    fetch_d.start()
+    weight.wait()
+    fetch_a.wait()
+    flat = grabbed[0].reshape(rows_here * cols, patch_len)
+    embedded[...], own[...] = embed_slot(flat, w_embed[...], gain_ref[...])
+    fetch_d.wait()
+
+
+def exchange_kernel(
     sample_ref,
     region_ref,
     a_gain_ref,
     o_gain_ref,
+    w_embed,
+    grabbed,
+    embedded_a,
+    own_a,
     store_ref,
-    w_embed_ref,
     w_qkv_ref,
     w_out_ref,
     w_dec_ref,
-    new_ref,
-    patches,
-    w_embed,
+    result,
     w_qkv,
     w_out,
     w_dec,
+    last_qkv,
+    last_far,
+    last_embedded,
+    last_final,
+    q_table,
+    k_table,
+    patches,
     embedded,
     own,
+    outgoing,
+    relay,
     far,
     own_qkv,
     finals,
     slot_sems,
     weight_sems,
+    relay_send_sems,
+    relay_recv_sems,
     send_sems,
     recv_sems,
 ):
@@ -256,61 +310,95 @@
     mine = lax.axis_index("lat") * lon_count + lax.axis_index("lon")
     other = lax.rem(mine + 2 * lax.rem(mine, 2) - 1 + strips, strips)
     partner = {"lat": lax.div(other, lon_count), "lon": lax.rem(other, lon_count)}
-
-    def slot_in(s):
-        return pltpu.make_async_copy(store_ref.at[s], patches.at[s], slot_sems.at[s])
-
+    peer = {"buf": 1 - lax.axis_index("buf")}
     tokens = rows_here * cols
     half = tokens // 2
     halves = [pl.ds(half * h, half) for h in range(2)]
-
-    def send(k, h):
+    windows = tokens // PER
+
+    barrier = pltpu.get_barrier_semaphore()
+    for device in (partner, peer):
+        pl.semaphore_signal(barrier, inc=1, device_id=device, device_id_type=MESH)
+
+    fetches = [
+        pltpu.make_async_copy(store_ref.at[s], patches.at[s], slot_sems.at[s])
+        for s in range(slots)
+    ]
+    for copy in fetches:
+        copy.start()
+    weights = [
+        pltpu.make_async_copy(src, dst, weight_sems.at[i])
+        for i, (src, dst) in enumerate(
+            ((w_qkv_ref, w_qkv), (w_out_ref, w_out), (w_dec_ref, w_dec))
+        )
+    ]
+    order, count = slot_order(sample_ref, slots)
+
+    def send(k, h, src, device):
         return pltpu.make_async_remote_copy(
-            src_ref=own.at[k, halves[h]],
+            src_ref=src,
             dst_ref=far.at[k, halves[h]],
             send_sem=send_sems.at[k, h],
             recv_sem=recv_sems.at[k, h],
-            device_id=partner,
-            device_id_type=pl.DeviceIdType.MESH,
-        )
-
-    weights = [
-        pltpu.make_async_copy(src, dst, weight_sems.at[i])
-        for i, (src, dst) in enumerate(
-            ((w_embed_ref, w_embed), (w_qkv_ref, w_qkv), (w_out_ref, w_out), (w_dec_ref, w_dec))
-        )
-    ]
-    weights[0].start()
-    slot_in(0).start()
-
-    barrier = pltpu.get_barrier_semaphore()
-    pl.semaphore_signal(
-        barrier, inc=1, device_id=partner, device_id_type=pl.DeviceIdType.MESH
-    )
+            device_id=device,
+            device_id_type=MESH,
+        )
+
+    def send_half(k, h):
+        src = own_a if k == UNIT_A else outgoing if k == UNIT_C else own.at[UNIT_B]
+        return send(k, h, src.at[halves[h]], partner)
+
+    def arrival(k, h):
+        return send(k, h, far.at[k, halves[h]], partner)
+
+    def forward(h):
+        return send(UNIT_D, h, far.at[UNIT_C, halves[h]], peer)
+
+    def relay_half(h):
+        return pltpu.make_async_remote_copy(
+            src_ref=own.at[UNIT_D, halves[h]],
+            dst_ref=relay.at[halves[h]],
+            send_sem=relay_send_sems.at[h],
+            recv_sem=relay_recv_sems.at[h],
+            device_id=peer,
+            device_id_type=MESH,
+        )
+
+    def embed(k, values):
+        flat = values.reshape(tokens, patch_len)
+        embedded[k], own[k] = embed_slot(flat, w_embed[...], a_gain_ref[...])
+
+    pl.semaphore_wait(barrier, 2)
+    for h in range(2):
+        send_half(UNIT_A, h).start()
+    embed(UNIT_D, grabbed[1])
+    for h in range(2):
+        relay_half(h).start()
+    embedded[UNIT_A] = embedded_a[...]
+    own[UNIT_A] = own_a[...]
     q_regions, k_regions = region_tables(
         region_ref[pl.ds(mine * HALF, HALF), :].astype(jnp.float32),
         region_ref[pl.ds(other * HALF, HALF), :].astype(jnp.float32),
     )
-    pl.semaphore_wait(barrier, 1)
+    q_table[...] = q_regions
+    k_table[...] = k_regions
+    for copy in fetches:
+        copy.wait()
+    for copy in weights:
+        copy.start()
+    embed(UNIT_C, patches[order[UNIT_C]])
+    embed(UNIT_B, patches[order[UNIT_B]])
+    result[UNIT_B] = patches[order[UNIT_B]]
+
+    for h in range(2):
+        relay_half(h).wait_recv()
+        at = slice(half * h, half * (h + 1))
+        outgoing[at] = jnp.where(count >= 3, own[UNIT_C, at], relay[at])
+        send_half(UNIT_C, h).start()
+    for h in range(2):
+        send_half(UNIT_B, h).start()
+
     weights[0].wait()
-    slot_in(0).wait()
-    for s in range(1, slots):
-        slot_in(s).start()
-    for copy in weights[1:]:
-        copy.start()
-
-    @pl.loop(0, slots)
-    def _(k):
-        @pl.when(k > 0)
-        def _():
-            slot_in(k).wait()
-
-        flat = patches[k].reshape(tokens, patch_len)
-        embedded[k], own[k] = embed_slot(flat, w_embed[...], a_gain_ref[...])
-        for h in range(2):
-            send(k, h).start()
-
-    weights[1].wait()
 
     @pl.loop(0, slots)
     def _(k):
@@ -320,44 +408,110 @@
             own[k], w_qkv[:, D:], preferred_element_type=jnp.float32
         ).astype(jnp.bfloat16)
 
+    weights[1].wait()
     weights[2].wait()
-    weights[3].wait()
-    windows = tokens // PER
-
-    @pl.loop(0, slots)
+
+    def mix_half(k, h):
+        at = slice(half * h, half * (h + 1))
+        here = slice(windows // 2 * h, windows // 2 * (h + 1))
+        kv_other = jnp.dot(far[k, at], w_qkv[:, D:], preferred_element_type=jnp.float32)
+        mixed = attend_slot(
+            own_qkv[k, at, :D],
+            own_qkv[k, at, D:],
+            kv_other.astype(jnp.bfloat16),
+            q_table[here, :],
+            k_table[:, here],
+        )
+        return finish_part(embedded[k, at], mixed, w_out[...], o_gain_ref[...])
+
+    @pl.loop(0, UNIT_B)
     def _(k):
         for h in range(2):
-            send(k, h).wait()
-            at = slice(half * h, half * (h + 1))
-            here = slice(windows // 2 * h, windows // 2 * (h + 1))
-            kv_other = jnp.dot(far[k, at], w_qkv[:, D:], preferred_element_type=jnp.float32)
-            mixed = attend_slot(
-                own_qkv[k, at, :D],
-                own_qkv[k, at, D:],
-                kv_other.astype(jnp.bfloat16),
-                q_regions[here],
-                k_regions[:, here],
-            )
-            finals[at] = finish_part(embedded[k, at], mixed, w_out[...], o_gain_ref[...])
+            arrival(k, h).wait_recv()
+
+            @pl.when(k == UNIT_C)
+            def _():
+                forward(h).start()
+
+            finals[half * h : half * (h + 1)] = mix_half(k, h)
         final = from_windows(finals[...]).astype(jnp.bfloat16)
-        slot = lax.axis_index("buf") * slots + k
-        taken = sample_ref[0] == slot
-        for b in range(1, sample_ref.shape[0]):
-            taken = jnp.logical_or(taken, sample_ref[b] == slot)
-        final = jnp.where(taken, final, jnp.zeros_like(final))
-        flat = patches[k].reshape(tokens, patch_len)
-        new_ref[k] = decode_slot(flat, final, w_dec[...]).reshape(rows_here, cols, patch_len)
-
-
-def place_kernel(result_ref, new_ref, sems):
-    slots, rows = new_ref.shape[:2]
+        needed = jnp.where(k == UNIT_A, 1, jnp.where(k == UNIT_C, 3, 4))
+        final = jnp.where(count >= needed, final, jnp.zeros_like(final))
+        place = jnp.where(
+            k == UNIT_A, order[UNIT_A], jnp.where(k == UNIT_C, order[UNIT_C], order[UNIT_D])
+        )
+        flat = patches[place].reshape(tokens, patch_len)
+        result[k] = decode_slot(flat, final, w_dec[...]).reshape(rows_here, cols, patch_len)
+
+    arrival(UNIT_B, 0).wait_recv()
+    last_final[...] = mix_half(UNIT_B, 0)
+    last_qkv[...] = own_qkv[UNIT_B, half:]
+    last_embedded[...] = embedded[UNIT_B, half:]
+    for h in range(2):
+        relay_half(h).wait_send()
+        send_half(UNIT_A, h).wait_send()
+        send_half(UNIT_C, h).wait_send()
+        send_half(UNIT_B, h).wait_send()
+        forward(h).wait_send()
+    arrival(UNIT_B, 1).wait_recv()
+    last_far[...] = far[UNIT_B, half:]
+
+
+def last_kernel(
+    sample_ref,
+    o_gain_ref,
+    result,
+    w_qkv,
+    w_out,
+    w_dec,
+    last_qkv,
+    last_far,
+    last_embedded,
+    last_final,
+    q_table,
+    k_table,
+    new_ref,
+    decoded,
+    finals,
+    sems,
+    row_sems,
+):
+    slots, rows_here, cols, patch_len = result.shape
+    order, _ = slot_order(sample_ref, slots)
     copies = [
-        pltpu.make_async_copy(result_ref.at[s, i], new_ref.at[s, i], sems.at[s, i])
-        for s in range(slots)
-        for i in range(rows)
+        pltpu.make_async_copy(result.at[k], new_ref.at[order[k]], sems.at[k])
+        for k in (UNIT_A, UNIT_C, UNIT_D)
     ]
     for copy in copies:
         copy.start()
+    tokens = rows_here * cols
+    half = tokens // 2
+    windows = tokens // PER
+    kv_other = jnp.dot(last_far[...], w_qkv[:, D:], preferred_element_type=jnp.float32)
+    mixed = attend_slot(
+        last_qkv[:, :D],
+        last_qkv[:, D:],
+        kv_other.astype(jnp.bfloat16),
+        q_table[windows // 2 :, :],
+        k_table[:, windows // 2 :],
+    )
+    finals[:half] = last_final[...]
+    finals[half:] = finish_part(last_embedded[...], mixed, w_out[...], o_gain_ref[...])
+    final = from_windows(finals[...]).astype(jnp.bfloat16)
+    rows = rows_here // 2
+    for h in range(2):
+        here = slice(rows * h, rows * (h + 1))
+        decoded[here] = decode_slot(
+            result[UNIT_B, here].reshape(half, patch_len),
+            final[half * h : half * (h + 1)],
+            w_dec[...],
+        ).reshape(rows, cols, patch_len)
+        copies.append(
+            pltpu.make_async_copy(
+                decoded.at[here], new_ref.at[order[UNIT_B], here], row_sems.at[h]
+            )
+        )
+        copies[-1].start()
     for copy in copies:
         copy.wait()
 
@@ -367,27 +521,58 @@
 ):
     slots, rows_here, cols, patch_len = store.shape
     tokens = rows_here * cols
+    half = tokens // 2
+    windows = tokens // PER
     held = lambda *shape: pltpu.VMEM(shape, jnp.bfloat16)
+    wide = lambda *shape: pltpu.VMEM(shape, jnp.float32)
     vmem = pl.BlockSpec(memory_space=pltpu.VMEM)
-    hbm = pl.BlockSpec(memory_space=pl.ANY)
-    result = pl.pallas_call(
-        fused_kernel,
-        in_specs=[pl.BlockSpec(memory_space=pltpu.SMEM), vmem, vmem, vmem] + [hbm] * 5,
-        out_specs=vmem,
-        out_shape=pltpu.VMEM(store.shape, store.dtype),
+    smem = pl.BlockSpec(memory_space=pltpu.SMEM)
+    hbm = pl.BlockSpec(memory_space=pltpu.HBM)
+    in_hbm = lambda array: pltpu.with_memory_space_constraint(array, pltpu.HBM)
+    store, w_embed, w_qkv, w_out = (in_hbm(array) for array in (store, w_embed, w_qkv, w_out))
+    w_dec_t = in_hbm(w_dec.T)
+    w_embed_held, grabbed, embedded_a, own_a = pl.pallas_call(
+        first_kernel,
+        in_specs=[smem, vmem, hbm, hbm],
+        out_specs=[vmem] * 4,
+        out_shape=[
+            held(*w_embed.shape),
+            held(2, *store.shape[1:]),
+            held(tokens, D),
+            held(tokens, D),
+        ],
+        scratch_shapes=[pltpu.SemaphoreType.DMA((3,))],
+        compiler_params=pltpu.CompilerParams(vmem_limit_bytes=FIRST_LIMIT),
+    )(sample_index, attn_gain[None], store, w_embed)
+    carried = pl.pallas_call(
+        exchange_kernel,
+        in_specs=[smem] + [vmem] * 7 + [hbm] * 4,
+        out_specs=[vmem] * 10,
+        out_shape=[
+            held(*store.shape),
+            held(*w_qkv.shape),
+            held(*w_out.shape),
+            held(*w_dec_t.shape),
+            held(half, 3 * D),
+            held(half, D),
+            held(half, D),
+            wide(half, D),
+            wide(windows, GROUP * PER),
+            wide(2 * PER, windows),
+        ],
         scratch_shapes=[
             held(*store.shape),
-            held(*w_embed.shape),
-            held(*w_qkv.shape),
-            held(*w_out.shape),
-            held(*w_dec.shape[::-1]),
             held(slots, tokens, D),
             held(slots, tokens, D),
+            held(tokens, D),
+            held(tokens, D),
             held(slots, tokens, D),
             held(slots, tokens, 3 * D),
-            pltpu.VMEM((tokens, D), jnp.float32),
+            wide(tokens, D),
             pltpu.SemaphoreType.DMA((slots,)),
-            pltpu.SemaphoreType.DMA((4,)),
+            pltpu.SemaphoreType.DMA((3,)),
+            pltpu.SemaphoreType.DMA((2,)),
+            pltpu.SemaphoreType.DMA((2,)),
             pltpu.SemaphoreType.DMA((slots, 2)),
             pltpu.SemaphoreType.DMA((slots, 2)),
         ],
@@ -399,24 +584,39 @@
         region_ids,
         attn_gain[None],
         out_gain[None],
+        w_embed_held,
+        grabbed,
+        embedded_a,
+        own_a,
         store,
-        w_embed,
         w_qkv,
         w_out,
-        w_dec.T,
+        w_dec_t,
     )
     return pl.pallas_call(
-        place_kernel,
-        in_specs=[hbm],
+        last_kernel,
+        in_specs=[smem] + [vmem] * 11,
         out_specs=hbm,
         out_shape=jax.ShapeDtypeStruct(store.shape, store.dtype),
-        scratch_shapes=[pltpu.SemaphoreType.DMA((slots, rows_here))],
-        compiler_params=pltpu.CompilerParams(vmem_limit_bytes=PICK_LIMIT),
-    )(result)
-
-
-def local(store, *rest):
-    return (local_strips if store.shape[1] == HALF else local_tiles)(store, *rest)
+        scratch_shapes=[
+            held(*store.shape[1:]),
+            wide(tokens, D),
+            pltpu.SemaphoreType.DMA((slots,)),
+            pltpu.SemaphoreType.DMA((2,)),
+        ],
+        compiler_params=pltpu.CompilerParams(vmem_limit_bytes=LAST_LIMIT),
+    )(sample_index, out_gain[None], *carried)
+
+
+def local(store, sample_index, *rest):
+    slots, rows_here = store.shape[:2]
+    strips = (
+        rows_here == HALF
+        and slots == 4
+        and lax.axis_size("buf") == 2
+        and sample_index.shape[0] == 6
+    )
+    return (local_strips if strips else local_tiles)(store, sample_index, *rest)
 
 
 def solution(mesh):

time: 34 us -> 34.9 us (1.026)
  Pallas kernels: 33.8 us -> 34.6 us
    pallas_call x2 -> x3, Pallas kernels: 33.8 us -> 34.6 us  [the longest x1 27.1 us: local_strips(): pl.pallas_call(exchange_kernel, in_specs=[smem] + [vmem] * 7 + [hbm] * 4,...]
where the time goes in v1:
time: 34.9 us; the launch traced here: 34.7 us
  Pallas kernels  34.6 us (99%)
    pallas_call x1, Pallas kernels, local_strips(): pl.pallas_call(exchange_kernel, in_specs=[smem] + [vmem] * 7 + [hbm] * 4,...  27.1 us
    pallas_call x1, Pallas kernels, local_strips(): pl.pallas_call(last_kernel, in_specs=[smem] + [vmem] * 11, out_specs=hbm,...  4.18 us
    pallas_call x1, Pallas kernels, local_strips(): pl.pallas_call(first_kernel, in_specs=[smem, vmem, hbm, hbm], out_specs=[...  3.37 us

profile of v1, /device:TPU:1, one launch (start us, length us, event | category | flops | bytes accessed | tf_op | source)
XLA Modules:
  0.0 34.7 jit_solution(14171953899413903358)
XLA Ops:
  0.0 0.0 copy-start
  0.0 0.0 copy-start.1
  0.0 0.0 copy-start.2
  0.0 0.0 copy-start.3
  0.0 3.4 %shard_map.91 = (bf16[1725,512]{1,0:T(8,128)(2,1)S(1)}, bf16[2,4,64,1725]{3,2,1,0:T(8,128)(2,1)S(1)}, bf16[256,512]{1,0:T(8,128)(2,1)S(1)}, bf16[256,512]{1,0:T(8,128)(2,1)S(1)}) custom-call(s32[6]{0:T(128)} %sample_ref.5, f32[1,512]{1,0:T(1,128)} %bitcast.3, bf16[4,4,64,1725]{3,2,1,0:T(8,128)(2,1)} %store_ref.3, bf16[1725,512]{1,0:T(8,128)(2,1)} %w_embed_ref.1), custom_call_target="tpu_custom_call" | custom-call | tf_op jit(solution)/shard_map/pallas_call | solution.py:534
  3.4 0.0 copy-done
  3.4 0.0 copy-done.1
  3.4 0.0 copy-done.2
  3.4 0.0 copy-done.3
  3.4 27.1 %shard_map.92 = (bf16[4,4,64,1725]{3,2,1,0:T(8,128)(2,1)S(1)}, bf16[512,1536]{1,0:T(8,128)(2,1)S(1)}, bf16[512,512]{1,0:T(8,128)(2,1)S(1)}, bf16[1725,512]{1,0:T...) custom-call(s32[6]{0:T(128)S(1)} %copy-done.3, ...), custom_call_target="tpu_custom_call" | custom-call | tf_op jit(solution)/shard_map/pallas_call | solution.py:547
  30.5 4.2 %shard_map.93 = bf16[4,4,64,1725]{3,2,1,0:T(8,128)(2,1)} custom-call(s32[6]{0:T(128)S(1)} %copy-done.3, f32[1,512]{1,0:T(1,128)S(1)} %bitcast.6, bf16[4,4,64,1725]{3,2,1,0:T(8,128)(2,1)S(1)} %get-tuple-element.23.result, bf16[512,1536]{1,0:T(8,128)(2,1)S(1)} %get-tuple-element.24.w_qkv, bf16[512,512]{1,0:T(8,128)(2,1)S(1)} %get-tuple-element.25.w_out, ...), custom_call_target="tpu_custom_call" | custom-call | tf_op jit(solution)/shard_map/pallas_call | solution.py:596
Async XLA Ops:
  0.0 3.4 %copy-start = (s32[64,64]{1,0:T(8,128)S(1)}, s32[64,64]{1,0:T(8,128)}, u32[]{:S(2)}) copy-start(s32[64,64]{1,0:T(8,128)} %region_ref.1) | copy-start | bytes 49156
  0.0 3.4 %copy-start.1 = (f32[512]{0:T(512)S(1)}, f32[512]{0:T(512)}, u32[]{:S(2)}) copy-start(f32[512]{0:T(512)} %param.13) | copy-start | bytes 6148
  0.0 3.4 %copy-start.2 = (f32[512]{0:T(512)S(1)}, f32[512]{0:T(512)}, u32[]{:S(2)}) copy-start(f32[512]{0:T(512)} %param.16) | copy-start | bytes 6148
  0.0 3.4 %copy-start.3 = (s32[6]{0:T(128)S(1)}, s32[6]{0:T(128)}, u32[]{:S(2)}) copy-start(s32[6]{0:T(128)} %sample_ref.5) | copy-start | bytes 76

commit v2 on v1

--- a/solution.py
+++ b/solution.py
@@ -249,20 +249,26 @@
 
 
 def first_kernel(
-    sample_ref, gain_ref, store_ref, w_embed_ref, w_embed, grabbed, embedded, own, sems
+    sample_ref, gain_ref, store_ref, w_embed_ref, w_embed, grabbed, embedded, own, sample, gain, sems
 ):
     slots, rows_here, cols, patch_len = store_ref.shape
-    order, _ = slot_order(sample_ref, slots)
     weight = pltpu.make_async_copy(w_embed_ref, w_embed, sems.at[0])
+    sample_in = pltpu.make_async_copy(sample_ref, sample, sems.at[3])
+    gain_in = pltpu.make_async_copy(gain_ref, gain, sems.at[4])
+    sample_in.start()
+    weight.start()
+    gain_in.start()
+    sample_in.wait()
+    order, _ = slot_order(sample, slots)
     fetch_a = pltpu.make_async_copy(store_ref.at[order[UNIT_A]], grabbed.at[0], sems.at[1])
     fetch_d = pltpu.make_async_copy(store_ref.at[order[UNIT_D]], grabbed.at[1], sems.at[2])
-    weight.start()
     fetch_a.start()
+    gain_in.wait()
+    weight.wait()
     fetch_d.start()
-    weight.wait()
     fetch_a.wait()
     flat = grabbed[0].reshape(rows_here * cols, patch_len)
-    embedded[...], own[...] = embed_slot(flat, w_embed[...], gain_ref[...])
+    embedded[...], own[...] = embed_slot(flat, w_embed[...], gain[...])
     fetch_d.wait()
 
 
@@ -296,7 +302,6 @@
     relay,
     far,
     own_qkv,
-    finals,
     slot_sems,
     weight_sems,
     relay_send_sems,
@@ -311,10 +316,13 @@
     other = lax.rem(mine + 2 * lax.rem(mine, 2) - 1 + strips, strips)
     partner = {"lat": lax.div(other, lon_count), "lon": lax.rem(other, lon_count)}
     peer = {"buf": 1 - lax.axis_index("buf")}
+    near = lax.div(other, lon_count) == lax.axis_index("lat")
     tokens = rows_here * cols
     half = tokens // 2
-    halves = [pl.ds(half * h, half) for h in range(2)]
     windows = tokens // PER
+
+    def part(h):
+        return pl.ds(half * h if isinstance(h, int) else pl.multiple_of(half * h, half), half)
 
     barrier = pltpu.get_barrier_semaphore()
     for device in (partner, peer):
@@ -337,7 +345,7 @@
     def send(k, h, src, device):
         return pltpu.make_async_remote_copy(
             src_ref=src,
-            dst_ref=far.at[k, halves[h]],
+            dst_ref=far.at[k, part(h)],
             send_sem=send_sems.at[k, h],
             recv_sem=recv_sems.at[k, h],
             device_id=device,
@@ -346,18 +354,18 @@
 
     def send_half(k, h):
         src = own_a if k == UNIT_A else outgoing if k == UNIT_C else own.at[UNIT_B]
-        return send(k, h, src.at[halves[h]], partner)
+        return send(k, h, src.at[part(h)], partner)
 
     def arrival(k, h):
-        return send(k, h, far.at[k, halves[h]], partner)
+        return send(k, h, far.at[k, part(h)], partner)
 
     def forward(h):
-        return send(UNIT_D, h, far.at[UNIT_C, halves[h]], peer)
+        return send(UNIT_D, h, far.at[UNIT_C, part(h)], peer)
 
     def relay_half(h):
         return pltpu.make_async_remote_copy(
-            src_ref=own.at[UNIT_D, halves[h]],
-            dst_ref=relay.at[halves[h]],
+            src_ref=own.at[UNIT_D, part(h)],
+            dst_ref=relay.at[part(h)],
             send_sem=relay_send_sems.at[h],
             recv_sem=relay_recv_sems.at[h],
             device_id=peer,
@@ -390,30 +398,33 @@
     embed(UNIT_B, patches[order[UNIT_B]])
     result[UNIT_B] = patches[order[UNIT_B]]
 
-    for h in range(2):
-        relay_half(h).wait_recv()
-        at = slice(half * h, half * (h + 1))
-        outgoing[at] = jnp.where(count >= 3, own[UNIT_C, at], relay[at])
-        send_half(UNIT_C, h).start()
-    for h in range(2):
-        send_half(UNIT_B, h).start()
-
     weights[0].wait()
 
-    @pl.loop(0, slots)
-    def _(k):
+    def project(k):
         query = jnp.dot(own[k], w_qkv[:, :D], preferred_element_type=jnp.float32)
         own_qkv[k, :, :D] = (query * (1.0 / math.sqrt(HDIM))).astype(jnp.bfloat16)
         own_qkv[k, :, D:] = jnp.dot(
             own[k], w_qkv[:, D:], preferred_element_type=jnp.float32
         ).astype(jnp.bfloat16)
 
+    @pl.loop(0, 2)
+    def _(h):
+        project(2 * h)
+        project(2 * h + 1)
+        relay_half(h).wait_recv()
+        at = part(h)
+        outgoing[at] = jnp.where(count >= 3, own[UNIT_C, at], relay[at])
+        send_half(UNIT_C, h).start()
+
+    @pl.when(near)
+    def _():
+        for h in range(2):
+            send_half(UNIT_B, h).start()
+
     weights[1].wait()
     weights[2].wait()
 
-    def mix_half(k, h):
-        at = slice(half * h, half * (h + 1))
-        here = slice(windows // 2 * h, windows // 2 * (h + 1))
+    def mix(k, at, here):
         kv_other = jnp.dot(far[k, at], w_qkv[:, D:], preferred_element_type=jnp.float32)
         mixed = attend_slot(
             own_qkv[k, at, :D],
@@ -433,8 +444,7 @@
             def _():
                 forward(h).start()
 
-            finals[half * h : half * (h + 1)] = mix_half(k, h)
-        final = from_windows(finals[...]).astype(jnp.bfloat16)
+        final = from_windows(mix(k, slice(0, tokens), slice(0, windows))).astype(jnp.bfloat16)
         needed = jnp.where(k == UNIT_A, 1, jnp.where(k == UNIT_C, 3, 4))
         final = jnp.where(count >= needed, final, jnp.zeros_like(final))
         place = jnp.where(
@@ -443,8 +453,16 @@
         flat = patches[place].reshape(tokens, patch_len)
         result[k] = decode_slot(flat, final, w_dec[...]).reshape(rows_here, cols, patch_len)
 
-    arrival(UNIT_B, 0).wait_recv()
-    last_final[...] = mix_half(UNIT_B, 0)
+        @pl.when(jnp.logical_and(k == UNIT_A, jnp.logical_not(near)))
+        def _():
+            for h in range(2):
+                send_half(UNIT_B, h).start()
+
+        @pl.when(k == UNIT_C)
+        def _():
+            arrival(UNIT_B, 0).wait_recv()
+            last_final[...] = mix(UNIT_B, slice(0, half), slice(0, windows // 2))
+
     last_qkv[...] = own_qkv[UNIT_B, half:]
     last_embedded[...] = embedded[UNIT_B, half:]
     for h in range(2):
@@ -533,7 +551,7 @@
     w_dec_t = in_hbm(w_dec.T)
     w_embed_held, grabbed, embedded_a, own_a = pl.pallas_call(
         first_kernel,
-        in_specs=[smem, vmem, hbm, hbm],
+        in_specs=[hbm] * 4,
         out_specs=[vmem] * 4,
         out_shape=[
             held(*w_embed.shape),
@@ -541,9 +559,13 @@
             held(tokens, D),
             held(tokens, D),
         ],
-        scratch_shapes=[pltpu.SemaphoreType.DMA((3,))],
+        scratch_shapes=[
+            pltpu.SMEM(sample_index.shape, jnp.int32),
+            wide(1, D),
+            pltpu.SemaphoreType.DMA((5,)),
+        ],
         compiler_params=pltpu.CompilerParams(vmem_limit_bytes=FIRST_LIMIT),
-    )(sample_index, attn_gain[None], store, w_embed)
+    )(in_hbm(sample_index), in_hbm(attn_gain[None]), store, w_embed)
     carried = pl.pallas_call(
         exchange_kernel,
         in_specs=[smem] + [vmem] * 7 + [hbm] * 4,
@@ -568,7 +590,6 @@
             held(tokens, D),
             held(slots, tokens, D),
             held(slots, tokens, 3 * D),
-            wide(tokens, D),
             pltpu.SemaphoreType.DMA((slots,)),
             pltpu.SemaphoreType.DMA((3,)),
             pltpu.SemaphoreType.DMA((2,)),

time: 34.9 us -> 32.8 us (0.940)
  Pallas kernels: 34.6 us -> 32.6 us
    pallas_call x1, Pallas kernels: 27.1 us -> 25.4 us  [local_strips(): pl.pallas_call(exchange_kernel, in_specs=[smem] + [vmem] * 7 + [hbm] * 4,...]
    pallas_call x1, Pallas kernels: 3.37 us -> 3.02 us  [local_strips(): pl.pallas_call(first_kernel, in_specs=[hbm] * 4, out_specs=[vmem] * 4, ou...]
where the time goes in v2:
time: 32.8 us; the launch traced here: 32.7 us
  Pallas kernels  32.6 us (99%)
    pallas_call x1, Pallas kernels, local_strips(): pl.pallas_call(exchange_kernel, in_specs=[smem] + [vmem] * 7 + [hbm] * 4,...  25.4 us
    pallas_call x1, Pallas kernels, local_strips(): pl.pallas_call(last_kernel, in_specs=[smem] + [vmem] * 11, out_specs=hbm,...  4.18 us
    pallas_call x1, Pallas kernels, local_strips(): pl.pallas_call(first_kernel, in_specs=[hbm] * 4, out_specs=[vmem] * 4, ou...  3.02 us

profile of v2, /device:TPU:1, one launch (start us, length us, event | category | flops | bytes accessed | tf_op | source)
XLA Modules:
  0.0 32.7 jit_solution(15515029400440492871)
XLA Ops:
  0.0 0.0 copy-start
  0.0 0.0 copy-start.1
  0.0 0.0 copy-start.2
  0.0 0.0 copy-start.3
  0.0 3.0 %shard_map.91 = (bf16[1725,512]{1,0:T(8,128)(2,1)S(1)}, bf16[2,4,64,1725]{3,2,1,0:T(8,128)(2,1)S(1)}, bf16[256,512]{1,0:T(8,128)(2,1)S(1)}, bf16[256,512]{1,0:T(8,128)(2,1)S(1)}) custom-call(s32[6]{0:T(128)} %sample_ref.5, f32[1,512]{1,0:T(1,128)} %bitcast.3, bf16[4,4,64,1725]{3,2,1,0:T(8,128)(2,1)} %store_ref.3, bf16[1725,512]{1,0:T(8,128)(2,1)} %w_embed_ref.1), custom_call_target="tpu_custom_call" | custom-call | tf_op jit(solution)/shard_map/pallas_call | solution.py:552
  3.0 0.0 copy-done
  3.1 0.0 copy-done.1
  3.1 0.0 copy-done.2
  3.1 0.0 copy-done.3
  3.1 25.4 %shard_map.92 = (bf16[4,4,64,1725]{3,2,1,0:T(8,128)(2,1)S(1)}, bf16[512,1536]{1,0:T(8,128)(2,1)S(1)}, bf16[512,512]{1,0:T(8,128)(2,1)S(1)}, bf16[1725,512]{1,0:T...) custom-call(s32[6]{0:T(128)S(1)} %copy-done.3, ...), custom_call_target="tpu_custom_call" | custom-call | tf_op jit(solution)/shard_map/pallas_call | solution.py:569
  28.5 4.2 %shard_map.93 = bf16[4,4,64,1725]{3,2,1,0:T(8,128)(2,1)} custom-call(s32[6]{0:T(128)S(1)} %copy-done.3, f32[1,512]{1,0:T(1,128)S(1)} %bitcast.6, bf16[4,4,64,1725]{3,2,1,0:T(8,128)(2,1)S(1)} %get-tuple-element.23.result, bf16[512,1536]{1,0:T(8,128)(2,1)S(1)} %get-tuple-element.24.w_qkv, bf16[512,512]{1,0:T(8,128)(2,1)S(1)} %get-tuple-element.25.w_out, ...), custom_call_target="tpu_custom_call" | custom-call | tf_op jit(solution)/shard_map/pallas_call | solution.py:617
Async XLA Ops:
  0.0 3.1 %copy-start = (s32[64,64]{1,0:T(8,128)S(1)}, s32[64,64]{1,0:T(8,128)}, u32[]{:S(2)}) copy-start(s32[64,64]{1,0:T(8,128)} %region_ref.1) | copy-start | bytes 49156
  0.0 3.1 %copy-start.1 = (f32[512]{0:T(512)S(1)}, f32[512]{0:T(512)}, u32[]{:S(2)}) copy-start(f32[512]{0:T(512)} %param.13) | copy-start | bytes 6148
  0.0 3.1 %copy-start.2 = (f32[512]{0:T(512)S(1)}, f32[512]{0:T(512)}, u32[]{:S(2)}) copy-start(f32[512]{0:T(512)} %param.16) | copy-start | bytes 6148
  0.0 3.1 %copy-start.3 = (s32[6]{0:T(128)S(1)}, s32[6]{0:T(128)}, u32[]{:S(2)}) copy-start(s32[6]{0:T(128)} %sample_ref.5) | copy-start | bytes 76

commit v3 on v2

--- a/solution.py
+++ b/solution.py
@@ -232,9 +232,10 @@
 def slot_order(sample_ref, slots):
     first = lax.axis_index("buf") * slots
     taken = []
+    samples = len(sample_ref) if isinstance(sample_ref, list) else sample_ref.shape[0]
     for s in range(slots):
         hit = sample_ref[0] == first + s
-        for b in range(1, sample_ref.shape[0]):
+        for b in range(1, samples):
             hit = jnp.logical_or(hit, sample_ref[b] == first + s)
         taken.append(hit.astype(jnp.int32))
     count = sum(taken)
@@ -273,7 +274,7 @@
 
 
 def exchange_kernel(
-    sample_ref,
+    sample_in,
     region_ref,
     a_gain_ref,
     o_gain_ref,
@@ -286,15 +287,15 @@
     w_out_ref,
     w_dec_ref,
     result,
+    w_dec,
+    finals,
+    sample,
     w_qkv,
     w_out,
-    w_dec,
-    last_qkv,
-    last_far,
-    last_embedded,
-    last_final,
     q_table,
     k_table,
+    q_parts,
+    k_parts,
     patches,
     embedded,
     own,
@@ -332,7 +333,8 @@
         pltpu.make_async_copy(store_ref.at[s], patches.at[s], slot_sems.at[s])
         for s in range(slots)
     ]
-    for copy in fetches:
+    fetches.append(pltpu.make_async_copy(sample_in, sample, slot_sems.at[slots]))
+    for copy in reversed(fetches):
         copy.start()
     weights = [
         pltpu.make_async_copy(src, dst, weight_sems.at[i])
@@ -340,12 +342,10 @@
             ((w_qkv_ref, w_qkv), (w_out_ref, w_out), (w_dec_ref, w_dec))
         )
     ]
-    order, count = slot_order(sample_ref, slots)
-
-    def send(k, h, src, device):
+    def send(k, h, at, src, device):
         return pltpu.make_async_remote_copy(
-            src_ref=src,
-            dst_ref=far.at[k, part(h)],
+            src_ref=src.at[at],
+            dst_ref=far.at[k, at],
             send_sem=send_sems.at[k, h],
             recv_sem=recv_sems.at[k, h],
             device_id=device,
@@ -353,14 +353,16 @@
         )
 
     def send_half(k, h):
-        src = own_a if k == UNIT_A else outgoing if k == UNIT_C else own.at[UNIT_B]
-        return send(k, h, src.at[part(h)], partner)
+        return send(k, h, part(h), own_a if k == UNIT_A else outgoing, partner)
+
+    def send_piece(q):
+        return send(UNIT_B, q, part(q), own.at[UNIT_B], partner)
 
     def arrival(k, h):
-        return send(k, h, far.at[k, part(h)], partner)
+        return send(k, h, part(h), far.at[k], partner)
 
     def forward(h):
-        return send(UNIT_D, h, far.at[UNIT_C, part(h)], peer)
+        return send(UNIT_D, h, part(h), far.at[UNIT_C], peer)
 
     def relay_half(h):
         return pltpu.make_async_remote_copy(
@@ -390,10 +392,15 @@
     )
     q_table[...] = q_regions
     k_table[...] = k_regions
+    each = windows // 2
+    for q in range(2):
+        q_parts[q] = q_regions[each * q : each * (q + 1)]
+        k_parts[q] = k_regions[:, each * q : each * (q + 1)]
     for copy in fetches:
         copy.wait()
     for copy in weights:
         copy.start()
+    order, count = slot_order(sample, slots)
     embed(UNIT_C, patches[order[UNIT_C]])
     embed(UNIT_B, patches[order[UNIT_B]])
     result[UNIT_B] = patches[order[UNIT_B]]
@@ -418,103 +425,78 @@
 
     @pl.when(near)
     def _():
-        for h in range(2):
-            send_half(UNIT_B, h).start()
+        for q in range(2):
+            send_piece(q).start()
 
     weights[1].wait()
     weights[2].wait()
 
-    def mix(k, at, here):
+    def mix(k, at, q_regions, k_regions):
         kv_other = jnp.dot(far[k, at], w_qkv[:, D:], preferred_element_type=jnp.float32)
         mixed = attend_slot(
             own_qkv[k, at, :D],
             own_qkv[k, at, D:],
             kv_other.astype(jnp.bfloat16),
-            q_table[here, :],
-            k_table[:, here],
+            q_regions,
+            k_regions,
         )
         return finish_part(embedded[k, at], mixed, w_out[...], o_gain_ref[...])
 
-    @pl.loop(0, UNIT_B)
-    def _(k):
-        for h in range(2):
-            arrival(k, h).wait_recv()
-
-            @pl.when(k == UNIT_C)
+    @pl.loop(0, 5)
+    def _(step):
+        whole = jnp.logical_or(step < 2, step == 3)
+
+        @pl.when(whole)
+        def _():
+            k = jnp.minimum(step, UNIT_D)
+            for h in range(2):
+                arrival(k, h).wait_recv()
+
+                @pl.when(k == UNIT_C)
+                def _():
+                    forward(h).start()
+
+            mixed = mix(k, pl.ds(0, tokens), q_table[...], k_table[...])
+            final = from_windows(mixed).astype(jnp.bfloat16)
+            needed = jnp.where(k == UNIT_A, 1, jnp.where(k == UNIT_C, 3, 4))
+            final = jnp.where(count >= needed, final, jnp.zeros_like(final))
+            place = jnp.where(
+                k == UNIT_A, order[UNIT_A], jnp.where(k == UNIT_C, order[UNIT_C], order[UNIT_D])
+            )
+            flat = patches[place].reshape(tokens, patch_len)
+            result[k] = decode_slot(flat, final, w_dec[...]).reshape(rows_here, cols, patch_len)
+
+            @pl.when(jnp.logical_and(k == UNIT_A, jnp.logical_not(near)))
             def _():
-                forward(h).start()
-
-        final = from_windows(mix(k, slice(0, tokens), slice(0, windows))).astype(jnp.bfloat16)
-        needed = jnp.where(k == UNIT_A, 1, jnp.where(k == UNIT_C, 3, 4))
-        final = jnp.where(count >= needed, final, jnp.zeros_like(final))
-        place = jnp.where(
-            k == UNIT_A, order[UNIT_A], jnp.where(k == UNIT_C, order[UNIT_C], order[UNIT_D])
-        )
-        flat = patches[place].reshape(tokens, patch_len)
-        result[k] = decode_slot(flat, final, w_dec[...]).reshape(rows_here, cols, patch_len)
-
-        @pl.when(jnp.logical_and(k == UNIT_A, jnp.logical_not(near)))
+                for q in range(2):
+                    send_piece(q).start()
+
+        @pl.when(jnp.logical_not(whole))
         def _():
-            for h in range(2):
-                send_half(UNIT_B, h).start()
-
-        @pl.when(k == UNIT_C)
-        def _():
-            arrival(UNIT_B, 0).wait_recv()
-            last_final[...] = mix(UNIT_B, slice(0, half), slice(0, windows // 2))
-
-    last_qkv[...] = own_qkv[UNIT_B, half:]
-    last_embedded[...] = embedded[UNIT_B, half:]
+            q = (step - 2) // 2
+            send_piece(q).wait_recv()
+            finals[part(q)] = mix(UNIT_B, part(q), q_parts[q], k_parts[q])
+
     for h in range(2):
         relay_half(h).wait_send()
         send_half(UNIT_A, h).wait_send()
         send_half(UNIT_C, h).wait_send()
-        send_half(UNIT_B, h).wait_send()
         forward(h).wait_send()
-    arrival(UNIT_B, 1).wait_recv()
-    last_far[...] = far[UNIT_B, half:]
-
-
-def last_kernel(
-    sample_ref,
-    o_gain_ref,
-    result,
-    w_qkv,
-    w_out,
-    w_dec,
-    last_qkv,
-    last_far,
-    last_embedded,
-    last_final,
-    q_table,
-    k_table,
-    new_ref,
-    decoded,
-    finals,
-    sems,
-    row_sems,
-):
+    for q in range(2):
+        send_piece(q).wait_send()
+
+
+def last_kernel(sample_ref, result, w_dec, finals, new_ref, decoded, sems, row_sems):
     slots, rows_here, cols, patch_len = result.shape
-    order, _ = slot_order(sample_ref, slots)
+    samples = sample_ref[...]
+    order, _ = slot_order([samples[0, b] for b in range(samples.shape[1])], slots)
     copies = [
         pltpu.make_async_copy(result.at[k], new_ref.at[order[k]], sems.at[k])
         for k in (UNIT_A, UNIT_C, UNIT_D)
     ]
     for copy in copies:
         copy.start()
-    tokens = rows_here * cols
-    half = tokens // 2
-    windows = tokens // PER
-    kv_other = jnp.dot(last_far[...], w_qkv[:, D:], preferred_element_type=jnp.float32)
-    mixed = attend_slot(
-        last_qkv[:, :D],
-        last_qkv[:, D:],
-        kv_other.astype(jnp.bfloat16),
-        q_table[windows // 2 :, :],
-        k_table[:, windows // 2 :],
-    )
-    finals[:half] = last_final[...]
-    finals[half:] = finish_part(last_embedded[...], mixed, w_out[...], o_gain_ref[...])
+    half = rows_here * cols // 2
     final = from_windows(finals[...]).astype(jnp.bfloat16)
     rows = rows_here // 2
     for h in range(2):
@@ -539,15 +521,14 @@
 ):
     slots, rows_here, cols, patch_len = store.shape
     tokens = rows_here * cols
-    half = tokens // 2
     windows = tokens // PER
     held = lambda *shape: pltpu.VMEM(shape, jnp.bfloat16)
     wide = lambda *shape: pltpu.VMEM(shape, jnp.float32)
     vmem = pl.BlockSpec(memory_space=pltpu.VMEM)
-    smem = pl.BlockSpec(memory_space=pltpu.SMEM)
     hbm = pl.BlockSpec(memory_space=pltpu.HBM)
     in_hbm = lambda array: pltpu.with_memory_space_constraint(array, pltpu.HBM)
-    store, w_embed, w_qkv, w_out = (in_hbm(array) for array in (store, w_embed, w_qkv, w_out))
+    samples, sample_index, store = sample_index, in_hbm(sample_index), in_hbm(store)
+    w_embed, w_qkv, w_out = in_hbm(w_embed), in_hbm(w_qkv), in_hbm(w_out)
     w_dec_t = in_hbm(w_dec.T)
     w_embed_held, grabbed, embedded_a, own_a = pl.pallas_call(
         first_kernel,
@@ -565,24 +546,24 @@
             pltpu.SemaphoreType.DMA((5,)),
         ],
         compiler_params=pltpu.CompilerParams(vmem_limit_bytes=FIRST_LIMIT),
-    )(in_hbm(sample_index), in_hbm(attn_gain[None]), store, w_embed)
+    )(sample_index, in_hbm(attn_gain[None]), store, w_embed)
     carried = pl.pallas_call(
         exchange_kernel,
-        in_specs=[smem] + [vmem] * 7 + [hbm] * 4,
-        out_specs=[vmem] * 10,
+        in_specs=[hbm] + [vmem] * 7 + [hbm] * 4,
+        out_specs=[vmem] * 3,
         out_shape=[
             held(*store.shape),
+            held(*w_dec_t.shape),
+            wide(tokens, D),
+        ],
+        scratch_shapes=[
+            pltpu.SMEM(sample_index.shape, jnp.int32),
             held(*w_qkv.shape),
             held(*w_out.shape),
-            held(*w_dec_t.shape),
-            held(half, 3 * D),
-            held(half, D),
-            held(half, D),
-            wide(half, D),
             wide(windows, GROUP * PER),
             wide(2 * PER, windows),
-        ],
-        scratch_shapes=[
+            wide(2, windows // 2, GROUP * PER),
+            wide(2, 2 * PER, windows // 2),
             held(*store.shape),
             held(slots, tokens, D),
             held(slots, tokens, D),
@@ -590,7 +571,7 @@
             held(tokens, D),
             held(slots, tokens, D),
             held(slots, tokens, 3 * D),
-            pltpu.SemaphoreType.DMA((slots,)),
+            pltpu.SemaphoreType.DMA((slots + 1,)),
             pltpu.SemaphoreType.DMA((3,)),
             pltpu.SemaphoreType.DMA((2,)),
             pltpu.SemaphoreType.DMA((2,)),
@@ -616,17 +597,16 @@
     )
     return pl.pallas_call(
         last_kernel,
-        in_specs=[smem] + [vmem] * 11,
+        in_specs=[vmem] * 4,
         out_specs=hbm,
         out_shape=jax.ShapeDtypeStruct(store.shape, store.dtype),
         scratch_shapes=[
             held(*store.shape[1:]),
-            wide(tokens, D),
             pltpu.SemaphoreType.DMA((slots,)),
             pltpu.SemaphoreType.DMA((2,)),
         ],
         compiler_params=pltpu.CompilerParams(vmem_limit_bytes=LAST_LIMIT),
-    )(sample_index, out_gain[None], *carried)
+    )(samples[None], *carried)
 
 
 def local(store, sample_index, *rest):

time: 32.8 us -> 31.8 us (0.970)
  Pallas kernels: 32.6 us -> 31.5 us
    pallas_call x2, Pallas kernels: 29.6 us -> 28.5 us  [the longest x1 25.9 us: local_strips(): pl.pallas_call(exchange_kernel, in_specs=[hbm] + [vmem] * 7 + [hbm] * 4,...]
where the time goes in v3:
time: 31.8 us; the launch traced here: 31.6 us
  Pallas kernels  31.5 us (99%)
    pallas_call x1, Pallas kernels, local_strips(): pl.pallas_call(exchange_kernel, in_specs=[hbm] + [vmem] * 7 + [hbm] * 4,...  25.9 us
    pallas_call x1, Pallas kernels, local_strips(): pl.pallas_call(first_kernel, in_specs=[hbm] * 4, out_specs=[vmem] * 4, ou...  3.03 us
    pallas_call x1, Pallas kernels, local_strips(): pl.pallas_call(last_kernel, in_specs=[vmem] * 4, out_specs=hbm, out_shape...  2.6 us

profile of v3, /device:TPU:1, one launch (start us, length us, event | category | flops | bytes accessed | tf_op | source)
XLA Modules:
  0.0 31.6 jit_solution(4134170852099906110)
XLA Ops:
  0.0 0.0 copy-start
  0.0 0.0 copy-start.1
  0.0 0.0 copy-start.3
  0.0 3.0 %shard_map.91 = (bf16[1725,512]{1,0:T(8,128)(2,1)S(1)}, bf16[2,4,64,1725]{3,2,1,0:T(8,128)(2,1)S(1)}, bf16[256,512]{1,0:T(8,128)(2,1)S(1)}, bf16[256,512]{1,0:T(8,128)(2,1)S(1)}) custom-call(s32[6]{0:T(128)} %sample_in.1, f32[1,512]{1,0:T(1,128)} %bitcast.4, bf16[4,4,64,1725]{3,2,1,0:T(8,128)(2,1)} %store_ref.3, bf16[1725,512]{1,0:T(8,128)(2,1)} %w_embed_ref.1), custom_call_target="tpu_custom_call" | custom-call | tf_op jit(solution)/shard_map/pallas_call | solution.py:533
  3.0 0.0 copy-done
  3.1 0.0 copy-done.1
  3.1 0.0 copy-done.3
  3.1 0.0 copy-start.2
  3.1 25.9 %shard_map.92 = (bf16[4,4,64,1725]{3,2,1,0:T(8,128)(2,1)S(1)}, bf16[1725,512]{1,0:T(8,128)(2,1)S(1)}, f32[256,512]{1,0:T(8,128)S(1)}) custom-call(s32[6]{0:T(128)} %sample_in.1, s32[64,64]{1,0:T(8,128)S(1)} %copy-done, f32[1,512]{1,0:T(1,128)S(1)} %bitcast.5, f32[1,512]{1,0:T(1,128)S(1)} %bitcast.7, bf16[1725,512]{1,0:T(8,128)(2,1)S(1)} %get-tuple-element.12.w_embed, ...), custom_call_target="tpu_custom_call" | custom-call | tf_op jit(solution)/shard_map/pallas_call | solution.py:550
  29.0 0.0 copy-done.2
  29.0 2.6 %shard_map.93 = bf16[4,4,64,1725]{3,2,1,0:T(8,128)(2,1)} custom-call(s32[1,6]{1,0:T(1,128)S(1)} %bitcast.6, bf16[4,4,64,1725]{3,2,1,0:T(8,128)(2,1)S(1)} %get-tuple-element.16.result, bf16[1725,512]{1,0:T(8,128)(2,1)S(1)} %get-tuple-element.17.w_dec, f32[256,512]{1,0:T(8,128)S(1)} %get-tuple-element.18.finals), custom_call_target="tpu_custom_call" | custom-call | tf_op jit(solution)/shard_map/pallas_call | solution.py:598
Async XLA Ops:
  0.0 3.0 %copy-start = (s32[64,64]{1,0:T(8,128)S(1)}, s32[64,64]{1,0:T(8,128)}, u32[]{:S(2)}) copy-start(s32[64,64]{1,0:T(8,128)} %region_ref.1) | copy-start | bytes 49156
  0.0 3.1 %copy-start.1 = (f32[512]{0:T(512)S(1)}, f32[512]{0:T(512)}, u32[]{:S(2)}) copy-start(f32[512]{0:T(512)} %param.13) | copy-start | bytes 6148
  0.0 3.1 %copy-start.3 = (f32[512]{0:T(512)S(1)}, f32[512]{0:T(512)}, u32[]{:S(2)}) copy-start(f32[512]{0:T(512)} %param.16) | copy-start | bytes 6148
  3.1 25.9 %copy-start.2 = (s32[6]{0:T(128)S(1)}, s32[6]{0:T(128)}, u32[]{:S(2)}) copy-start(s32[6]{0:T(128)} %sample_in.1) | copy-start | bytes 76
